TPU v7x, 128 devices: a whole 4x4x4 slice. The times are simulated.
128 devices in a mesh: seq: 16 (over x, y_hi, core), res: 8 (over z, y_lo).
Axes of the slice: x: 4, y: 4 (y_hi: 2, y_lo: 2; y = y_hi * 2 + y_lo), z: 4, core: 2. Of those that a mesh axis runs over, the one named last changes fastest.
Arguments:
- left_alignment: bfloat16 [256, 256, 32], P('seq', 'res'), may hold values from -6 to 6
- right_alignment: bfloat16 [256, 256, 32], P('seq', 'res'), may hold values from -6 to 6
- alignment_mask: int32 [256, 256], P('seq', 'res'), may hold values from 0 to 1, as said below
- output_weight: bfloat16 [32, 32, 128], replicated, may hold values from -3 to 3
- output_bias: float32 [128], replicated, may hold values from -4 to 4
- pair_update_cotangent: bfloat16 [256, 256, 128], P('seq', 'res'), may hold values from -6 to 6
Outputs:
- pair_update: bfloat16 [256, 256, 128], P('seq', 'res')
- left_operand_gradient: float32 [256, 256, 32], P('seq', 'res')
- right_operand_gradient: float32 [256, 256, 32], P('seq', 'res')
- weight_grad: float32 [32, 32, 128], replicated
- bias_grad: float32 [128], replicated
Inputs may be any that keep to these rules, and one draw needn't show every extreme that they name: alignment_mask is 0 or 1; sequence 0 is 1 at every residue.
All inputs are finite; a program needn't handle non-finite values.
Results may differ from a plain program's by a relative error of at most 0.0049.
Values may be sent and summed in bfloat16 or wider, within the bound.
No kernel may reach another device: no remote copies, remote signals or barrier semaphores. Data moves between devices by JAX's collectives and lax.ppermute only.
A program may use at most 256 MiB of HBM per device.

v0:
```python
import jax
import jax.numpy as jnp
from jax import lax
from jax.sharding import PartitionSpec as P


def per_device(
    left_alignment,
    right_alignment,
    alignment_mask,
    output_weight,
    output_bias,
    pair_update_cotangent,
):
    local_sequences, local_residues, channel_count = left_alignment.shape
    pair_ch = output_weight.shape[2]
    row_block = pair_update_cotangent.shape[0]
    mask_float = alignment_mask.astype(jnp.float32)
    mask_bfloat = alignment_mask.astype(jnp.bfloat16)
    left_under_mask = left_alignment * mask_bfloat[:, :, None]
    right_under_mask = right_alignment * mask_bfloat[:, :, None]
    projected = jnp.einsum(
        "sjd,cdh->scjh", right_under_mask, output_weight, preferred_element_type=jnp.float32
    ).astype(jnp.bfloat16)
    proj_flat = projected.reshape(local_sequences * channel_count, local_residues * pair_ch)
    full_mask = lax.all_gather(alignment_mask, "res", axis=1, tiled=True)
    left_all = lax.all_gather(left_under_mask, "res", axis=1, tiled=True)
    residues = left_all.shape[1]
    left_rows = left_all.transpose(1, 0, 2).reshape(residues, local_sequences * channel_count)
    count_terms = jnp.dot(
        full_mask.astype(jnp.float32).T, mask_float, precision=lax.Precision.HIGHEST
    )
    counts = (
        lax.psum_scatter(
            count_terms.astype(jnp.bfloat16), "seq", scatter_dimension=0, tiled=True
        ).astype(jnp.float32)
        + 0.001
    )
    picked = left_rows
    summed = lax.psum_scatter(
        jnp.dot(picked, proj_flat, preferred_element_type=jnp.float32).reshape(
            row_block * lax.axis_size("seq"), local_residues, pair_ch
        ),
        "seq",
        scatter_dimension=0,
        tiled=True,
    )
    pair_update = (summed / counts[:, :, None] + output_bias).astype(jnp.bfloat16)
    scaled = (pair_update_cotangent.astype(jnp.float32) / counts[:, :, None]).astype(jnp.bfloat16)
    portion = lax.all_gather(scaled, "seq", axis=0, tiled=True)
    height = portion.shape[0]
    flat = portion.reshape(height, local_residues * pair_ch)
    picked = left_rows
    grad_acc = lax.dot_general(
        picked, flat, (((0,), (0,)), ((), ())), preferred_element_type=jnp.float32
    )
    left_piece = lax.dot_general(
        flat, proj_flat, (((1,), (1,)), ((), ())), preferred_element_type=jnp.float32
    )
    left_sum = lax.psum_scatter(left_piece, "res", scatter_dimension=0, tiled=True)
    left_operand_gradient = (
        left_sum.reshape(local_residues, local_sequences, channel_count).transpose(1, 0, 2)
        * mask_float[:, :, None]
    )
    grad_four = grad_acc.reshape(local_sequences, channel_count, local_residues, pair_ch)
    weight32 = output_weight.astype(jnp.float32)
    right_operand_gradient = (
        jnp.einsum("scjh,cdh->sjd", grad_four, weight32, precision=lax.Precision.HIGHEST)
        * mask_float[:, :, None]
    )
    weight_terms = jnp.einsum(
        "sjd,scjh->cdh",
        right_under_mask.astype(jnp.float32),
        grad_four,
        precision=lax.Precision.HIGHEST,
    )
    bias_terms = jnp.sum(pair_update_cotangent.astype(jnp.float32), axis=(0, 1))
    weight_grad, bias_grad = lax.psum((weight_terms, bias_terms), ("seq", "res"))
    return (pair_update, left_operand_gradient, right_operand_gradient, weight_grad, bias_grad)


def solution(mesh):
    return jax.shard_map(
        per_device,
        mesh=mesh,
        in_specs=(
            P("seq", "res", None),
            P("seq", "res", None),
            P("seq", "res"),
            P(),
            P(),
            P("seq", "res", None),
        ),
        out_specs=(P("seq", "res", None), P("seq", "res", None), P("seq", "res", None), P(), P()),
        check_vma=False,
    )
```

profile of v0, /device:TPU:1, one launch (start us, length us, event | category | flops | bytes accessed | tf_op | source)
XLA Modules:
  0.0 477.2 jit_solution(3804345761741627732)
XLA Ops:
  7.2 24.7 %all-gather = s32[8,32,16]{1,2,0:T(8,128)S(1)} all-gather(s32[1,32,16]{1,2,0:T(8,128)} %bitcast.72), channel_id=1, replica_groups=mesh['seq'=16,'res'=8] {'res'}, dimensions={0}, use_global_device_ids=true | all-gather | bytes 18432 | tf_op jit(solution)/shard_map/all_gather | solution.py:26
  31.9 0.1 reshape.37
  32.0 1.7 convolution_convert_fusion.1
  33.8 0.0 reduce-scatter.4.cloned.1.call-start
  33.8 0.8 fusion.25
  34.6 0.1 copy.34
  34.7 1.1 fusion.23
  35.8 26.7 %all_gather.9 = bf16[16,256,32]{2,0,1:T(8,128)(2,1)S(1)} all-gather(bf16[16,32,32]{2,0,1:T(8,128)(2,1)S(1)} %get-tuple-element.26), channel_id=1, replica_groups=mesh['seq'=16,'res'=8] {'res'}, dimensions={1}, use_global_device_ids=true | all-gather | bytes 294912 | tf_op jit(solution)/shard_map/all_gather | solution.py:27
  62.5 0.8 copy.36
  63.3 1.2 convolution_convert_fusion
  64.6 6.2 %copy.87 = bf16[64,8,32,128]{3,1,2,0:T(8,128)(2,1)} copy(bf16[64,8,32,128]{3,2,1,0:T(8,128)(2,1)S(1)} %bitcast.67) | data formatting | bytes 8388608
  70.8 6.5 %copy.39 = bf16[4096,512]{1,0:T(8,128)(2,1)} copy(bf16[4096,512]{0,1:T(8,128)(2,1)} %bitcast.69) | data formatting | bytes 8388608 | tf_op jit(solution)/shard_map/dot_general | solution.py:41
  77.3 5.5 %fusion.26 = f32[256,32,128]{2,0,1:T(8,128)} fusion(bf16[256,512,1]{0,1,2:T(8,128)(2,1)S(1)} %bitcast.71, bf16[32,128,512]{2,1,0:T(8,128)(2,1)} %bitcast.66), kind=kOutput, calls=%fused_computation.30 | convolution fusion | flops 1073741824 | bytes 8650752 | tf_op jit(solution)/shard_map/dot_general | solution.py:41
  82.8 17.7 %reduce-scatter.6.cloned.1.call-done = bf16[16,32]{1,0:T(8,128)(2,1)} async-done(((bf16[256,32]{1,0:T(8,128)(2,1)}), bf16[16,32]{1,0:T(8,128)(2,1)}) %reduce-scatter.6.cloned.1.call-update) | async-done | bytes 1040 | tf_op jit(solution)/shard_map/reduce_scatter | solution.py:34
  100.6 0.7 convert_add_fusion
  101.2 0.1 copy.42
  101.3 83.3 %reduce-scatter.4.cloned.1.call-done = f32[16,32,128]{2,0,1:T(8,128)} async-done(((f32[256,32,128]{2,0,1:T(8,128)}), f32[16,32,128]{2,0,1:T(8,128)}) %reduce-scatter.4.cloned.1.call-update) | async-done | bytes 262160 | tf_op jit(solution)/shard_map/reduce_scatter | solution.py:40
  184.7 1.7 convert_reduce_fusion
  186.4 0.2 reduce-scatter.8.cloned.1.call-start
  186.7 51.4 %all-gather.3.cloned.1.call-done = bf16[256,32,128]{2,0,1:T(8,128)(2,1)} async-done(((bf16[16,32,128]{2,0,1:T(8,128)(2,1)}), bf16[256,32,128]{2,0,1:T(8,128)(2,1)}) %all-gather.3.cloned.1.call-update) | async-done | bytes 2097168 | tf_op jit(solution)/shard_map/all_gather | solution.py:50
  238.0 3.3 copy.44
  241.3 5.7 %fusion.4 = f32[256,512]{1,0:T(8,128)} fusion(bf16[256,4096]{0,1:T(8,128)(2,1)S(1)} %bitcast.70, bf16[64,8,32,128]{3,2,1,0:T(8,128)(2,1)} %bitcast.68), kind=kOutput, calls=%fused_computation.4 | convolution fusion | flops 1073741824 | bytes 6815744 | tf_op jit(solution)/shard_map/dot_general | solution.py:57
  247.1 0.7 copy.49
  247.8 64.9 %psum.15 = f32[128]{0:T(128)} all-reduce(f32[128]{0:T(128)S(1)} %get-tuple-element.20), channel_id=1, replica_groups=mesh['seq'=16,'res'=8] {'seq','res'}, use_global_device_ids=true, to_apply=%region_5.0 | all-reduce | flops 128 | bytes 1024 | tf_op jit(solution)/shard_map/psum | solution.py:78
  312.7 1.3 fusion.7
  314.0 3.2 copy-done.1
  317.3 8.7 %fusion.9 = f32[32,32,128]{2,1,0:T(8,128)} fusion(bf16[16,32,32,1]{2,0,1,3:T(8,128)(2,1)S(1)} %get-tuple-element.25, f32[16,32,32,128]{3,1,2,0:T(8,128)S(1)} %fusion.7), kind=kOutput, calls=%fused_computation.11 | convolution fusion | flops 805306368 | bytes 8945664 | tf_op jit(solution)/shard_map/sjd,scjh->cdh/dot_general | solution.py:71
  326.0 10.4 %fusion.15 = f32[16,32,32]{2,1,0:T(8,128)} fusion(f32[16,32,32,128]{3,1,2,0:T(8,128)} %copy-done.1, bf16[32,32,128]{2,1,0:T(8,128)(2,1)S(1)} %copy-done, f32[16,32]{1,0:T(8,128)S(1)} %get-tuple-element.23), kind=kOutput, calls=%fused_computation.13 | convolution fusion | flops 805322752 | bytes 8718336 | tf_op jit(solution)/shard_map/scjh,cdh->sjd/dot_general | solution.py:68
  336.4 1.0 reshape.34
  337.4 0.8 bitcast_multiply_fusion
  338.2 130.6 %all-reduce.2.cloned.1.call-done = f32[32,32,128]{2,1,0:T(8,128)} async-done(((f32[32,32,128]{2,1,0:T(8,128)}), f32[32,32,128]{2,1,0:T(8,128)}) %all-reduce.2.cloned.1.call-update) | async-done | bytes 524304 | tf_op jit(solution)/shard_map/psum | solution.py:78
  468.8 1.9 copy.89
  (20 shorter events, 0.3 us)
Async XLA Ops:
  7.2 56.2 %copy-start = (bf16[32,32,128]{2,1,0:T(8,128)(2,1)S(1)}, bf16[32,32,128]{2,1,0:T(8,128)(2,1)}, u32[]{:S(2)}) copy-start(bf16[32,32,128]{2,1,0:T(8,128)(2,1)} %param.9) | copy-start | bytes 786436
  7.2 93.4 %reduce-scatter.6.cloned.1.call-start = ((), (), s32[]{:S(2)}) async-start(), calls=%async_computation.4 | async-start | bytes 69632 | tf_op jit(solution)/shard_map/reduce_scatter | solution.py:34
  33.8 150.9 %reduce-scatter.4.cloned.1.call-start = ((), (), s32[]{:S(2)}) async-start(), calls=%async_computation.3 | async-start | bytes 4456448 | tf_op jit(solution)/shard_map/reduce_scatter | solution.py:40
  64.6 6.3 %copy-start.2 = (bf16[16,32,32,128]{3,1,2,0:T(8,128)(2,1)}, bf16[16,32,32,128]{3,1,2,0:T(8,128)(2,1)S(1)}, u32[]{:S(2)}) copy-start(bf16[16,32,32,128]{3,1,2,0:T(8,128)(2,1)S(1)} %convolution_convert_fusion) | copy-start | bytes 12582916
  82.8 101.9 %copy-start.3 = (bf16[16,32,128]{2,1,0:T(8,128)(2,1)S(1)}, bf16[16,32,128]{2,1,0:T(8,128)(2,1)}, u32[]{:S(2)}) copy-start(bf16[16,32,128]{2,1,0:T(8,128)(2,1)} %param.11) | copy-start | bytes 393220
  82.8 101.9 %copy-start.4 = (f32[128]{0:T(128)S(1)}, f32[128]{0:T(128)}, u32[]{:S(2)}) copy-start(f32[128]{0:T(128)} %param.10) | copy-start | bytes 1540
  82.8 155.2 %all-gather.3.cloned.1.call-start = ((), (), s32[]{:S(2)}) async-start(), calls=%async_computation.5 | async-start | bytes 2228224 | tf_op jit(solution)/shard_map/all_gather | solution.py:50
  186.4 150.0 %reduce-scatter.8.cloned.1.call-start = ((), (), s32[]{:S(2)}) async-start(), calls=%async_computation.6 | async-start | bytes 589824 | tf_op jit(solution)/shard_map/reduce_scatter | solution.py:60
  247.1 221.8 %all-reduce.2.cloned.1.call-start = ((), (), s32[]{:S(2)}) async-start(), calls=%async_computation.7 | async-start | bytes 1048576 | tf_op jit(solution)/shard_map/psum | solution.py:78
  314.0 3.2 copy-start.1
Sparse Core Ops, SparseCore 0:
  33.9 66.6 reduce-scatter.5
  104.6 79.9 reduce-scatter.3
  187.7 50.2 all-gather.2
  247.2 31.7 reduce-scatter.7
  326.1 142.6 all-reduce.1
where the time goes:
time: 478 us; the launch traced here: 477 us
  waiting for transfers between devices  283 us (59%)
  blocking collectives  116 us (24%)
  matrix products  34.6 us (7%)
  local copies, waits for them, and re-layouts  23.8 us (5%)
  between operations  13.9 us (3%)
  other arithmetic  5.16 us (1%)
    psum x1, waiting for transfers between devices, per_device(): lax.psum((weight_terms, bias_terms), ('seq', 'res'))  131 us
    reduce_scatter x1, waiting for transfers between devices, per_device(): lax.psum_scatter(jnp.dot(picked, proj_flat, preferred_element_type=jnp.fl...  83.3 us
    psum x1, blocking collectives, per_device(): lax.psum((weight_terms, bias_terms), ('seq', 'res'))  64.9 us
    all_gather x1, waiting for transfers between devices, per_device(): portion = lax.all_gather(scaled, 'seq', axis=0, tiled=True)  51.4 us
    all_gather x1, blocking collectives, per_device(): left_all = lax.all_gather(left_under_mask, 'res', axis=1, tiled=True)  26.7 us
    all_gather x1, blocking collectives, per_device(): full_mask = lax.all_gather(alignment_mask, 'res', axis=1, tiled=True)  24.7 us
    reduce_scatter x1, waiting for transfers between devices, per_device(): lax.psum_scatter(count_terms.astype(jnp.bfloat16), 'seq', scatter_dimensi...  17.7 us
    unnamed x13, local copies, waits for them, and re-layouts  12 us
  transfers between devices with their start and end apart: 5, of which 4 were waited for; matrix products, arithmetic and copies ran while one was open for 10% of the time, Pallas kernels for 0%

commit v1 on v0

--- a/solution.py
+++ b/solution.py
@@ -75,7 +75,7 @@
         precision=lax.Precision.HIGHEST,
     )
     bias_terms = jnp.sum(pair_update_cotangent.astype(jnp.float32), axis=(0, 1))
-    weight_grad, bias_grad = lax.psum((weight_terms, bias_terms), ("seq", "res"))
+    weight_grad, bias_grad = lax.psum(lax.psum((weight_terms, bias_terms), "res"), "seq")
     return (pair_update, left_operand_gradient, right_operand_gradient, weight_grad, bias_grad)
 
 

time: 478 us -> 518 us (1.084)
  waiting for transfers between devices: 283 us -> 336 us
  blocking collectives: 116 us -> 104 us
    reduce_scatter x1, waiting for transfers between devices: 0.01 us -> 29.5 us  [per_device(): lax.psum_scatter(left_piece, 'res', scatter_dimension=0, tiled=True)]
    psum x1 -> x2, waiting for transfers between devices: 131 us -> 154 us  [the longest x1 143 us: per_device(): lax.psum(lax.psum((weight_terms, bias_terms), 'res'), 'seq')]
    psum x1 -> x2, blocking collectives: 64.9 us -> 52.3 us  [the longest x1 36.5 us: per_device(): lax.psum(lax.psum((weight_terms, bias_terms), 'res'), 'seq')]
  transfers between devices with their start and end apart: 5 -> 6, of which waited for: 4 -> 6; matrix products, arithmetic and copies ran while one was open for 10% -> 8% of each run, Pallas kernels for 0% -> 0%
where the time goes in v1:
time: 518 us
  waiting for transfers between devices  336 us (65%)
  blocking collectives  104 us (20%)
  matrix products  34.3 us (7%)
  local copies, waits for them, and re-layouts  23.9 us (5%)
  between operations  14.2 us (3%)
    psum x1, waiting for transfers between devices, per_device(): lax.psum(lax.psum((weight_terms, bias_terms), 'res'), 'seq')  143 us
    reduce_scatter x1, waiting for transfers between devices, per_device(): lax.psum_scatter(jnp.dot(picked, proj_flat, preferred_element_type=jnp.fl...  83.3 us
    all_gather x1, waiting for transfers between devices, per_device(): portion = lax.all_gather(scaled, 'seq', axis=0, tiled=True)  51.4 us
    psum x1, blocking collectives, per_device(): lax.psum(lax.psum((weight_terms, bias_terms), 'res'), 'seq')  36.5 us
    reduce_scatter x1, waiting for transfers between devices, per_device(): lax.psum_scatter(left_piece, 'res', scatter_dimension=0, tiled=True)  29.5 us
    all_gather x1, blocking collectives, per_device(): left_all = lax.all_gather(left_under_mask, 'res', axis=1, tiled=True)  26.7 us
    all_gather x1, blocking collectives, per_device(): full_mask = lax.all_gather(alignment_mask, 'res', axis=1, tiled=True)  24.7 us
    reduce_scatter x1, waiting for transfers between devices, per_device(): lax.psum_scatter(count_terms.astype(jnp.bfloat16), 'seq', scatter_dimensi...  17.7 us
  transfers between devices with their start and end apart: 6, of which 6 were waited for; matrix products, arithmetic and copies ran while one was open for 8% of the time, Pallas kernels for 0%

profile of v1, /device:TPU:1, one launch (start us, length us, event | category | flops | bytes accessed | tf_op | source)
XLA Modules:
  0.0 517.8 jit_solution(11137973249865470984)
XLA Ops:
  7.2 24.7 %all-gather = s32[8,32,16]{1,2,0:T(8,128)S(1)} all-gather(s32[1,32,16]{1,2,0:T(8,128)} %bitcast.72), channel_id=1, replica_groups=mesh['seq'=16,'res'=8] {'res'}, dimensions={0}, use_global_device_ids=true | all-gather | bytes 18432 | tf_op jit(solution)/shard_map/all_gather | solution.py:26
  32.0 1.7 convolution_convert_fusion.1
  33.8 0.8 fusion.25
  34.7 1.1 fusion.23
  35.8 26.7 %all_gather.9 = bf16[16,256,32]{2,0,1:T(8,128)(2,1)S(1)} all-gather(bf16[16,32,32]{2,0,1:T(8,128)(2,1)S(1)} %get-tuple-element.26), channel_id=1, replica_groups=mesh['seq'=16,'res'=8] {'res'}, dimensions={1}, use_global_device_ids=true | all-gather | bytes 294912 | tf_op jit(solution)/shard_map/all_gather | solution.py:27
  62.5 0.8 copy.36
  63.3 1.2 convolution_convert_fusion
  64.6 6.2 %copy.87 = bf16[64,8,32,128]{3,1,2,0:T(8,128)(2,1)} copy(bf16[64,8,32,128]{3,2,1,0:T(8,128)(2,1)S(1)} %bitcast.67) | data formatting | bytes 8388608
  70.8 6.5 %copy.39 = bf16[4096,512]{1,0:T(8,128)(2,1)} copy(bf16[4096,512]{0,1:T(8,128)(2,1)} %bitcast.69) | data formatting | bytes 8388608 | tf_op jit(solution)/shard_map/dot_general | solution.py:41
  77.3 5.4 %fusion.26 = f32[256,32,128]{2,0,1:T(8,128)} fusion(bf16[256,512,1]{0,1,2:T(8,128)(2,1)S(1)} %bitcast.71, bf16[32,128,512]{2,1,0:T(8,128)(2,1)} %bitcast.66), kind=kOutput, calls=%fused_computation.30 | convolution fusion | flops 1073741824 | bytes 8650752 | tf_op jit(solution)/shard_map/dot_general | solution.py:41
  82.8 17.7 %reduce-scatter.6.cloned.1.call-done = bf16[16,32]{1,0:T(8,128)(2,1)} async-done(((bf16[256,32]{1,0:T(8,128)(2,1)}), bf16[16,32]{1,0:T(8,128)(2,1)}) %reduce-scatter.6.cloned.1.call-update) | async-done | bytes 1040 | tf_op jit(solution)/shard_map/reduce_scatter | solution.py:34
  100.6 0.7 convert_add_fusion
  101.3 83.3 %reduce-scatter.4.cloned.1.call-done = f32[16,32,128]{2,0,1:T(8,128)} async-done(((f32[256,32,128]{2,0,1:T(8,128)}), f32[16,32,128]{2,0,1:T(8,128)}) %reduce-scatter.4.cloned.1.call-update) | async-done | bytes 262160 | tf_op jit(solution)/shard_map/reduce_scatter | solution.py:40
  184.7 1.7 convert_reduce_fusion
  186.4 0.2 all-reduce.3.cloned.1.call-start
  186.7 51.4 %all-gather.3.cloned.1.call-done = bf16[256,32,128]{2,0,1:T(8,128)(2,1)} async-done(((bf16[16,32,128]{2,0,1:T(8,128)(2,1)}), bf16[256,32,128]{2,0,1:T(8,128)(2,1)}) %all-gather.3.cloned.1.call-update) | async-done | bytes 2097168 | tf_op jit(solution)/shard_map/all_gather | solution.py:50
  238.0 3.3 copy.44
  241.3 1.3 fusion.7
  242.6 3.2 copy-done.1
  245.8 8.7 %fusion.9 = f32[32,32,128]{2,1,0:T(8,128)} fusion(bf16[16,32,32,1]{2,0,1,3:T(8,128)(2,1)S(1)} %get-tuple-element.25, f32[16,32,32,128]{3,1,2,0:T(8,128)S(1)} %fusion.7), kind=kOutput, calls=%fused_computation.11 | convolution fusion | flops 805306368 | bytes 8945664 | tf_op jit(solution)/shard_map/sjd,scjh->cdh/dot_general | solution.py:71
  254.6 5.7 %fusion.4 = f32[256,512]{1,0:T(8,128)} fusion(bf16[256,4096]{0,1:T(8,128)(2,1)S(1)} %bitcast.70, bf16[64,8,32,128]{3,2,1,0:T(8,128)(2,1)} %bitcast.68), kind=kOutput, calls=%fused_computation.4 | convolution fusion | flops 1073741824 | bytes 6815744 | tf_op jit(solution)/shard_map/dot_general | solution.py:57
  260.4 0.3 all-reduce.5.cloned.1.call-start
  260.7 0.7 copy.49
  261.3 15.8 %psum.30 = f32[128]{0:T(128)S(1)} all-reduce(f32[128]{0:T(128)S(1)} %get-tuple-element.20), channel_id=1, replica_groups=mesh['seq'=16,'res'=8] {'res'}, use_global_device_ids=true, to_apply=%region_6.0 | all-reduce | flops 128 | bytes 1024 | tf_op jit(solution)/shard_map/psum | solution.py:78
  277.2 36.5 %psum.31 = f32[128]{0:T(128)} all-reduce(f32[128]{0:T(128)S(1)} %psum.30), channel_id=1, replica_groups=mesh['seq'=16,'res'=8] {'seq'}, use_global_device_ids=true, to_apply=%region_7.0 | all-reduce | flops 128 | bytes 1024 | tf_op jit(solution)/shard_map/psum | solution.py:78
  313.7 10.9 %all-reduce.3.cloned.1.call-done = f32[32,32,128]{2,1,0:T(8,128)} async-done(((f32[32,32,128]{2,1,0:T(8,128)}), f32[32,32,128]{2,1,0:T(8,128)}) %all-reduce.3.cloned.1.call-update) | async-done | bytes 524304 | tf_op jit(solution)/shard_map/psum | solution.py:78
  324.6 10.2 %fusion.15 = f32[16,32,32]{2,1,0:T(8,128)} fusion(f32[16,32,32,128]{3,1,2,0:T(8,128)} %copy-done.1, bf16[32,32,128]{2,1,0:T(8,128)(2,1)S(1)} %copy-done, f32[16,32]{1,0:T(8,128)S(1)} %get-tuple-element.23), kind=kOutput, calls=%fused_computation.13 | convolution fusion | flops 805322752 | bytes 8718336 | tf_op jit(solution)/shard_map/scjh,cdh->sjd/dot_general | solution.py:68
  334.8 29.5 %reduce-scatter.8.cloned.1.call-done = f32[32,512]{1,0:T(8,128)} async-done(((f32[256,512]{1,0:T(8,128)}), f32[32,512]{1,0:T(8,128)}) %reduce-scatter.8.cloned.1.call-update) | async-done | bytes 65552 | tf_op jit(solution)/shard_map/reduce_scatter | solution.py:60
  364.3 0.9 reshape.34
  365.3 0.8 bitcast_multiply_fusion
  366.1 142.9 %all-reduce.5.cloned.1.call-done = f32[32,32,128]{2,1,0:T(8,128)} async-done(((f32[32,32,128]{2,1,0:T(8,128)}), f32[32,32,128]{2,1,0:T(8,128)}) %all-reduce.5.cloned.1.call-update) | async-done | bytes 524304 | tf_op jit(solution)/shard_map/psum | solution.py:78
  509.0 1.9 copy.90
  (24 shorter events, 0.6 us)
Async XLA Ops:
  7.2 56.2 %copy-start = (bf16[32,32,128]{2,1,0:T(8,128)(2,1)S(1)}, bf16[32,32,128]{2,1,0:T(8,128)(2,1)}, u32[]{:S(2)}) copy-start(bf16[32,32,128]{2,1,0:T(8,128)(2,1)} %param.9) | copy-start | bytes 786436
  7.2 93.4 %reduce-scatter.6.cloned.1.call-start = ((), (), s32[]{:S(2)}) async-start(), calls=%async_computation.4 | async-start | bytes 69632 | tf_op jit(solution)/shard_map/reduce_scatter | solution.py:34
  33.8 150.9 %reduce-scatter.4.cloned.1.call-start = ((), (), s32[]{:S(2)}) async-start(), calls=%async_computation.3 | async-start | bytes 4456448 | tf_op jit(solution)/shard_map/reduce_scatter | solution.py:40
  64.6 6.2 %copy-start.2 = (bf16[16,32,32,128]{3,1,2,0:T(8,128)(2,1)}, bf16[16,32,32,128]{3,1,2,0:T(8,128)(2,1)S(1)}, u32[]{:S(2)}) copy-start(bf16[16,32,32,128]{3,1,2,0:T(8,128)(2,1)S(1)} %convolution_convert_fusion) | copy-start | bytes 12582916
  82.7 101.9 %copy-start.3 = (bf16[16,32,128]{2,1,0:T(8,128)(2,1)S(1)}, bf16[16,32,128]{2,1,0:T(8,128)(2,1)}, u32[]{:S(2)}) copy-start(bf16[16,32,128]{2,1,0:T(8,128)(2,1)} %param.11) | copy-start | bytes 393220
  82.7 101.9 %copy-start.4 = (f32[128]{0:T(128)S(1)}, f32[128]{0:T(128)}, u32[]{:S(2)}) copy-start(f32[128]{0:T(128)} %param.10) | copy-start | bytes 1540
  82.8 155.3 %all-gather.3.cloned.1.call-start = ((), (), s32[]{:S(2)}) async-start(), calls=%async_computation.5 | async-start | bytes 2228224 | tf_op jit(solution)/shard_map/all_gather | solution.py:50
  186.4 138.1 %all-reduce.3.cloned.1.call-start = ((), (), s32[]{:S(2)}) async-start(), calls=%async_computation.7 | async-start | bytes 1048576 | tf_op jit(solution)/shard_map/psum | solution.py:78
  242.6 3.2 copy-start.1
  254.6 109.7 %reduce-scatter.8.cloned.1.call-start = ((), (), s32[]{:S(2)}) async-start(), calls=%async_computation.6 | async-start | bytes 589824 | tf_op jit(solution)/shard_map/reduce_scatter | solution.py:60
  260.4 248.7 %all-reduce.5.cloned.1.call-start = ((), (), s32[]{:S(2)}) async-start(), calls=%async_computation.8 | async-start | bytes 1048576 | tf_op jit(solution)/shard_map/psum | solution.py:78
Sparse Core Ops, SparseCore 0:
  33.9 66.6 reduce-scatter.5
  104.6 79.9 reduce-scatter.3
  187.7 50.2 all-gather.2
  254.7 69.8 all-reduce.2
  327.3 36.9 reduce-scatter.7
  366.8 142.2 all-reduce.4
